TPU v7x, 128 devices: a whole 4x4x4 slice. The times are simulated.
128 devices in a mesh: seq: 16 (over x, y), mp: 8 (over z, core).
Axes of the slice: x: 4, y: 4, z: 4, core: 2. Of those that a mesh axis runs over, the one named last changes fastest.
Arguments:
- tokens: bfloat16 [16, 16, 64, 1024], P('seq'), may hold values from -25 to 25
- proj_main: bfloat16 [1024, 2, 2048], P('seq', None, 'mp'), may hold values from -0.1875 to 0.1875
- proj_shared: bfloat16 [1024, 2, 128], P('seq'), may hold values from -0.0078125 to 0.0078125
- proj_step: bfloat16 [1024, 32], P('seq', 'mp'), may hold values from -0.1875 to 0.1875
- step_bias: float32 [32], P('mp'), may hold values from -1.5 to 0.5
- decay_rate: float32 [2, 32], P(None, 'mp'), as said below
- skip_gain: float32 [32], P('mp'), may hold values from -1 to 2
- cotangent: bfloat16 [16, 16, 64, 2048], P('seq', None, None, 'mp'), may hold values from -6 to 6
Outputs:
- gated: bfloat16 [16, 16, 64, 2048], P('seq', None, None, 'mp')
- input_grad: bfloat16 [16, 16, 64, 1024], P('seq', None, None, 'mp')
- grad_main: float32 [1024, 2, 2048], P('seq', None, 'mp')
- grad_shared: float32 [1024, 2, 128], P('seq')
- grad_step: float32 [1024, 32], P('seq', 'mp')
Inputs may be any that keep to these rules, and one draw needn't show every extreme that they name: `decay_rate`: positive decay rates.
All inputs are finite; a program needn't handle non-finite values.
Results may differ from a plain program's by a relative error of at most 0.023.
Values may be sent and summed in bfloat16 or wider, within the bound.
A program may use at most 256 MiB of HBM per device.

v0:
```python
import jax
import jax.numpy as jnp
from jax import lax
from jax.experimental import pallas as pl
from jax.experimental.pallas import tpu as pltpu
from jax.sharding import PartitionSpec as P

MESH = pl.DeviceIdType.MESH
BF = jnp.bfloat16
F32 = jnp.float32

SEQ = 16
MP = 8
TOK = 1024
WID = 64
DM = 1024
INNER = 256
HEADS = 4
STATE = 128
LANES = 128
CHUNK = 256
CHUNKS = TOK // CHUNK
COLS = CHUNK // SEQ
SHARD = DM // SEQ
BX, BY, BB, BC, ROWS_L, ROWS = 0, 2, 4, 5, 256, 272
PIECE = STATE // SEQ
HALF = 3 * LANES
LOG2E = 1.4426950408889634


def iota(shape, axis):
    return lax.broadcasted_iota(jnp.int32, shape, axis)


def mm(a, b):
    return lax.dot_general(a, b, (((1,), (0,)), ((), ())), preferred_element_type=F32)


def mm_nt(a, b):
    return lax.dot_general(a, b, (((1,), (1,)), ((), ())), preferred_element_type=F32)


def mm_tn(a, b):
    return lax.dot_general(a, b, (((0,), (0,)), ((), ())), preferred_element_type=F32)


def halves(v):
    hi = v.astype(BF)
    return hi, (v - hi.astype(F32)).astype(BF)


def as_pair(v):
    lane = iota(v.shape, 1)
    hi = v.astype(BF).astype(F32)
    return jnp.where(lane < 4, hi, jnp.where(lane < 8, v - hi, 0.0)).astype(BF)


def fori(low, high, step):
    def run(i, carry):
        step(i)
        return carry

    lax.fori_loop(low, high, run, 0)


class SeqExchange:
    def __init__(self, source, landing, sems):
        self.source, self.landing = source, landing
        self.send, self.recv = sems
        self.me = lax.axis_index("seq")

    def copy(self, d):
        peer = lax.rem(self.me + d, SEQ)
        return pltpu.make_async_remote_copy(
            src_ref=self.source(peer),
            dst_ref=self.landing(self.me),
            send_sem=self.send.at[d],
            recv_sem=self.recv.at[d],
            device_id={"seq": peer},
            device_id_type=MESH,
        )

    def arrival(self, d):
        origin = lax.rem(self.me - d + SEQ, SEQ)
        return pltpu.make_async_remote_copy(
            src_ref=self.landing(origin),
            dst_ref=self.landing(origin),
            send_sem=self.send.at[d],
            recv_sem=self.recv.at[d],
            device_id={"seq": origin},
            device_id_type=MESH,
        )

    def start(self):
        fori(1, SEQ, lambda d: self.copy(d).start())

    def wait_recv(self):
        fori(1, SEQ, lambda d: self.arrival(d).wait_recv())

    def wait_send(self):
        fori(1, SEQ, lambda d: self.copy(d).wait_send())


class Ring:
    def __init__(self, me, to, whole, part, sems):
        self.whole, self.part, self.sems, self.to = whole, part, sems, to
        self.me, self.right, self.left = me, lax.rem(me + 1, 4), lax.rem(me + 3, 4)
        self.far = lax.rem(me + 2, 4)

    def copy(self, ref, k, peer):
        return pltpu.make_async_remote_copy(
            src_ref=ref,
            dst_ref=ref,
            send_sem=self.sems.at[0, k],
            recv_sem=self.sems.at[1, k],
            device_id={"seq": self.to(peer)},
            device_id_type=MESH,
        )

    def start(self):
        self.copy(self.whole(self.me), 0, self.right).start()
        self.copy(self.whole(self.me), 1, self.left).start()

    def forward(self):
        self.copy(self.whole(self.left), 0, self.left).wait_recv()
        self.copy(self.part(self.left, 0), 2, self.right).start()
        self.copy(self.whole(self.right), 1, self.right).wait_recv()
        self.copy(self.part(self.right, 1), 3, self.left).start()

    def finish(self):
        self.copy(self.part(self.far, 0), 2, self.left).wait_recv()
        self.copy(self.part(self.far, 1), 3, self.right).wait_recv()

    def wait_send(self):
        self.copy(self.whole(self.me), 0, self.right).wait_send()
        self.copy(self.whole(self.me), 1, self.left).wait_send()
        self.copy(self.part(self.left, 0), 2, self.right).wait_send()
        self.copy(self.part(self.right, 1), 3, self.left).wait_send()


class RingSum:
    def __init__(self, me, to, part, raw, near, sems):
        self.part, self.raw, self.near, self.sems, self.to = part, raw, near, sems, to
        self.me, self.far = me, lax.rem(me + 2, 4)
        self.side = (lax.rem(me + 3, 4), lax.rem(me + 1, 4))

    def copy(self, source, landing, k, peer):
        return pltpu.make_async_remote_copy(
            src_ref=source,
            dst_ref=landing,
            send_sem=self.sems.at[0, k],
            recv_sem=self.sems.at[1, k],
            device_id=self.to(peer),
            device_id_type=MESH,
        )

    def far_copy(self, n):
        return self.copy(self.part(self.far, n), self.raw(n), n, self.side[1 - n])

    def own_copy(self, n):
        peer = self.side[1 - n]
        return self.copy(self.part(peer, 1 - n), self.near(n, 1 - n), 2 + n, peer)

    def sum_copy(self, n):
        peer = self.side[1 - n]
        return self.copy(self.part(peer, n), self.near(n, n), 4 + n, peer)

    def start_far(self):
        for n in range(2):
            self.far_copy(n).start()

    def start_near(self):
        for n in range(2):
            self.own_copy(n).start()

    def middle(self):
        for n in range(2):
            self.copy(self.raw(n), self.raw(n), n, self.side[n]).wait_recv()
            ref = self.part(self.side[1 - n], n)
            ref[...] = (ref[...].astype(F32) + self.raw(n)[...].astype(F32)).astype(BF)
            self.sum_copy(n).start()

    def finish(self):
        halves = []
        for n in range(2):
            for k in range(2):
                ref = self.near(k, n)
                self.copy(ref, ref, 2 + k if n != k else 4 + k, self.side[k]).wait_recv()
            v = self.part(self.me, n)[...].astype(F32)
            halves.append(v + self.near(0, n)[...].astype(F32) + self.near(1, n)[...].astype(F32))
        return halves

    def wait_send(self):
        for n in range(2):
            self.far_copy(n).wait_send()
            self.own_copy(n).wait_send()
            self.sum_copy(n).wait_send()


def mp_copy(source, landing, send, recv, peer):
    return pltpu.make_async_remote_copy(
        src_ref=source,
        dst_ref=landing,
        send_sem=send,
        recv_sem=recv,
        device_id={"mp": peer},
        device_id_type=MESH,
    )


class MpExchange:
    def __init__(self, source, landing, sems):
        self.source, self.landing = source, landing
        self.send, self.recv = sems
        self.me = lax.axis_index("mp")

    def copy(self, d):
        peer = lax.rem(self.me + d, MP)
        return mp_copy(self.source(peer), self.landing(self.me), self.send.at[d], self.recv.at[d], peer)

    def arrival(self, d):
        origin = lax.rem(self.me - d + MP, MP)
        ref = self.landing(origin)
        return mp_copy(ref, ref, self.send.at[d], self.recv.at[d], origin)

    def start(self):
        fori(1, MP, lambda d: self.copy(d).start())

    def wait_recv(self):
        fori(1, MP, lambda d: self.arrival(d).wait_recv())

    def wait_send(self):
        fori(1, MP, lambda d: self.copy(d).wait_send())


def scan_scratch():
    v = pltpu.VMEM
    return dict(
        xs=v((CHUNKS, CHUNK, INNER), BF),
        xt=v((CHUNKS, CHUNK, INNER), BF),
        ed=v((CHUNKS, CHUNK, INNER), BF),
        er=v((CHUNKS, CHUNK, INNER), F32),
        tail=v((CHUNKS, CHUNK, INNER), F32),
        rcol=v((CHUNKS, CHUNK, LANES), F32),
        fresh=v((CHUNKS, STATE, INNER), F32),
        back=v((CHUNKS, STATE, INNER), F32),
        eR=v((CHUNKS, 8, INNER), F32),
        RC=v((8, INNER), F32),
        st=v((SEQ, 4 * PIECE, INNER), BF),
        sx=v((SEQ, 4 * PIECE, INNER), BF),
        sy=v((SEQ, 2 * PIECE, INNER), BF),
        sz=v((SEQ, 2 * PIECE, INNER), BF),
        y=v((CHUNKS, CHUNK, INNER), F32),
        dx=v((CHUNKS, CHUNK, INNER), F32),
        dbc=v((CHUNKS, CHUNK, 2 * STATE), F32),
        dd=v((CHUNKS, CHUNK, LANES), F32),
        gin=v((CHUNKS, STATE, INNER), F32),
        sin=v((STATE, INNER), F32),
    )


def main_scratch():
    v = pltpu.VMEM
    dma = pltpu.SemaphoreType.DMA
    seq_sems = lambda: dma((2, SEQ))
    return dict(
        tok3=v((SEQ, WID, DM), BF),
        cot=v((TOK, INNER), BF),
        wa=v((4, 4, SHARD, HALF), BF),
        wb=v((4, 4, SHARD, HALF), BF),
        sw_rx=v((SEQ, 16, LANES), BF),
        sw=v((LANES, DM), BF),
        z=v((TOK, INNER), BF),
        sraw=v((TOK, LANES), F32),
        pay=v((SEQ, ROWS, LANES), BF),
        trx=v((SEQ, ROWS, LANES), BF),
        bpay=v((SEQ, ROWS, LANES), BF),
        brx=v((SEQ, ROWS, LANES), BF),
        tri=v((4, CHUNK, CHUNK), BF),
        lp=v((TOK, LANES), BF),
        bcr=v((2, SEQ, WID, LANES), BF),
        bct=v((2, SEQ, WID, LANES), BF),
        wx=v((DM, 2 * LANES), BF),
        tdb=v((2, CHUNKS, CHUNK, LANES), BF),
        trs=v((MP, CHUNK, LANES), BF),
        tpiece=v((SEQ, COLS, LANES), BF),
        rpiece=v((SEQ, COLS, LANES), BF),
        rdb=v((2, SEQ, WID, LANES), BF),
        rrs=v((MP, SEQ, COLS, LANES), BF),
        dpiece=v((SEQ, COLS, LANES), BF),
        lacc=v((CHUNK, LANES), F32),
        swp=v((16, LANES), BF),
        R=scan_scratch(),
        T=scan_scratch(),
        g=v((TOK, 768), BF),
        tokt=v((DM, TOK), BF),
        gp=v((4, 4, SHARD, 640), BF),
        g_raw=v((2, 2, 2, 32, 640), BF),
        g_near=v((2, 2, 4, 32, 640), BF),
        h_own=v((2, 4, 32, 640), BF),
        h_raw=v((2, 2, 16, 640), BF),
        h_near=v((2, 2, 32, 640), BF),
        z_raw=v((2, 2, CHUNK, LANES), BF),
        z_near=v((2, 2, 2 * CHUNK, LANES), BF),
        gs=v((MP, 16, LANES), BF),
        gs_rx=v((SEQ, 16, LANES), BF),
        ip=v((MP, TOK, LANES), BF),
        prx=v((4, TOK, LANES), BF),
        zs=v((4, TOK, LANES), BF),
        fsh=v((SHARD, LANES), F32),
        frx=v((MP, SHARD, LANES), F32),
        s_local=dma((4,)),
        s_w=dma((4, 2, 4)),
        s_sw=seq_sems(),
        s_pay=seq_sems(),
        s_sr=seq_sems(),
        s_st=seq_sems(),
        s_ur=seq_sems(),
        s_ut=seq_sems(),
        s_back=seq_sems(),
        s_back2=seq_sems(),
        s_gp=dma((4, 2, 6)),
        s_bc=seq_sems(),
        s_bp=seq_sems(),
        s_gs=seq_sems(),
        s_bm=dma((2, MP)),
        s_tr=dma((2, MP)),
        s_rr=dma((2, MP)),
        s_fin=dma((2, MP)),
        s_pair=dma((2, 4, CHUNKS)),
        s_z=dma((2, 2, 6)),
    )


def sems(ref):
    return ref.at[0], ref.at[1]


def head_sum():
    c, h = iota((INNER, LANES), 0), iota((INNER, LANES), 1)
    return jnp.where((h < 8) & ((h & 3) == (c >> 6)), 1.0, 0.0).astype(BF)


def pair_expand(shift):
    k, c = iota((LANES, INNER), 0) - shift, iota((LANES, INNER), 1)
    return jnp.where((k >= 0) & (k < 8) & ((k & 3) == (c >> 6)), 1.0, 0.0).astype(BF)


def pair_merge(shift):
    k, h = iota((LANES, LANES), 0) - shift, iota((LANES, LANES), 1)
    return jnp.where((k >= 0) & (k < 8) & (h < 8) & ((k & 3) == (h & 3)), 1.0, 0.0).astype(BF)


def pair_place(shift):
    k, lane = iota((LANES, LANES), 0), iota((LANES, LANES), 1)
    return jnp.where((k < 8) & (lane == k + shift), 1.0, 0.0).astype(BF)


def wide(load, block, q):
    return jnp.concatenate([load(block, q), load(block + 1, q)], axis=1)


def summary(b, tri, load, pair_of, rate, ratex, q):
    x = wide(load, BX, q).astype(F32)
    dy = wide(load, BY, q).astype(F32)
    pair, shift = pair_of(q)
    dexp = mm(pair, pair_expand(shift))
    logs = (-dexp * ratex).astype(BF)
    rexp = mm(tri, logs)
    b["rcol"][q] = mm(tri, (-mm(pair, pair_merge(shift)) * rate).astype(BF))
    total = jnp.sum(logs.astype(F32), axis=0, keepdims=True)
    er = jnp.exp2(rexp)
    tail = jnp.exp2(jnp.minimum(total - rexp, 0.0))
    xs = (x * dexp).astype(BF)
    xt = (xs.astype(F32) * tail).astype(BF)
    ed = (er * dy).astype(BF)
    b["er"][q] = er
    b["tail"][q] = tail
    b["xs"][q] = xs
    b["xt"][q] = xt
    b["ed"][q] = ed
    b["fresh"][q] = mm_tn(load(BB, q), xt)
    b["back"][q] = mm_tn(load(BC, q), ed)
    rows = jnp.broadcast_to(total, (8, INNER))
    b["eR"][q] = jnp.exp2(rows)
    b["RC"][...] += rows


def pack_states(b):
    e = [b["eR"][q][:1] for q in range(CHUNKS)]
    end = b["fresh"][0]
    for q in range(1, CHUNKS):
        end = end * e[q] + b["fresh"][q]
    first = b["back"][CHUNKS - 1]
    for q in range(CHUNKS - 2, -1, -1):
        first = first * e[q] + b["back"][q]
    rc = b["RC"][...]
    hi = rc.astype(BF).astype(F32)
    logs = jnp.concatenate([hi, rc - hi], axis=0).astype(BF)
    pieces = [v.reshape(SEQ, PIECE, INNER) for v in (end, first)]
    b["st"][:, pl.ds(0, 2 * PIECE), :] = jnp.concatenate(pieces, axis=1).astype(BF)
    for k in range(SEQ):
        b["st"][k, pl.ds(2 * PIECE, 2 * PIECE)] = logs


def chain_states(b):
    own = [b["sx"][k, pl.ds(0, 2 * PIECE)].astype(F32) for k in range(SEQ)]
    logs = [b["sx"][k, pl.ds(2 * PIECE, 2 * PIECE)].astype(F32) for k in range(SEQ)]
    decay = [jnp.exp2(v[:PIECE] + v[PIECE:]) for v in logs]
    state = [jnp.zeros((PIECE, INNER), F32)]
    grad = [jnp.zeros((PIECE, INNER), F32)]
    for k in range(SEQ - 1):
        state.append(state[k] * decay[k] + own[k][:PIECE])
        n = SEQ - 1 - k
        grad.append(grad[k] * decay[n] + own[n][PIECE:])
    for k in range(SEQ):
        b["sy"][k] = jnp.concatenate([state[k], grad[SEQ - 1 - k]], axis=0).astype(BF)


def entering_states(b):
    both = b["sz"][...].astype(F32)
    b["sin"][...] = both[:, :PIECE, :].reshape(STATE, INNER)
    grad = both[:, PIECE:, :].reshape(STATE, INNER)
    for q in range(CHUNKS - 1, -1, -1):
        b["gin"][q] = grad
        if q > 0:
            grad = grad * b["eR"][q][:1] + b["back"][q]


def head_rows(h):
    one = jnp.where((iota((16, INNER), 1) >> 6) == h, 1.0, 0.0).astype(BF)
    return jnp.concatenate([one] * (CHUNK // 16), axis=0)


def inside(b, tri, load, q):
    dy = wide(load, BY, q)
    bmat = load(BB, q)
    cmat = load(BC, q)
    xs = b["xs"][q]
    trif = tri.astype(F32)
    scores = mm_nt(cmat, bmat) * trif
    rcol = b["rcol"][q]
    rrow = rcol.T
    pairs = None
    ms, dys, xss = [], [], []
    for h in range(HEADS):
        decay = jnp.exp2(jnp.minimum(rcol[:, h : h + 1] - rrow[h : h + 1, :], 0.0))
        ms.append((decay * scores).astype(BF))
        mask = head_rows(h)
        dys.append(dy * mask)
        xss.append(xs * mask)
        term = decay * mm_nt(dys[h], xs)
        pairs = term if h == 0 else pairs + term
    dy4 = jnp.concatenate(dys, axis=0)
    y = mm(jnp.concatenate(ms, axis=1), jnp.concatenate(xss, axis=0))
    dxs = mm_tn(jnp.concatenate(ms, axis=0), dy4)
    pairs = (pairs * trif).astype(BF)
    b["y"][q] = y
    b["dx"][q] = dxs
    b["dbc"][q, :, pl.ds(0, STATE)] = mm_tn(pairs, cmat)
    b["dbc"][q, :, pl.ds(STATE, STATE)] = mm(pairs, bmat)


def outside(b, tri, tri_up, load, pair_of, rate, q, put):
    x = wide(load, BX, q).astype(F32)
    dy = wide(load, BY, q).astype(F32)
    bmat = load(BB, q)
    cmat = load(BC, q)
    pair, shift = pair_of(q)
    dexp = mm(pair, pair_expand(shift))
    xs = b["xs"][q].astype(F32)
    state = b["sin"][...]
    grad = b["gin"][q]
    state_b, grad_b = state.astype(BF), grad.astype(BF)
    sums = head_sum()
    y = b["y"][q] + b["er"][q] * mm(cmat, state_b)
    inner = b["dx"][q]
    outer = b["tail"][q] * mm(bmat, grad_b)
    dxs = inner + outer
    db = b["dbc"][q, :, pl.ds(0, STATE)] + mm_nt(b["xt"][q], grad_b)
    dc = b["dbc"][q, :, pl.ds(STATE, STATE)] + mm_nt(b["ed"][q], state_b)

    def by_head(v):
        return mm(v.astype(BF), sums)

    late = by_head(dy * y - xs * inner).astype(BF)
    early = by_head(xs * outer).astype(BF)
    decayed = b["eR"][q][:1] * state
    across = jnp.sum(decayed * grad, axis=0, keepdims=True)
    across = mm(jnp.broadcast_to(across, (16, INNER)).astype(BF), sums)[:1]
    dl = mm(tri_up, late) + mm(tri, early) - early.astype(F32) + across
    ddelta = by_head(x * dxs) - rate * dl
    b["sin"][...] = decayed + b["fresh"][q]
    put(q, y, dexp * dxs, db, dc, ddelta)


def kernel(tok_hbm, cot_hbm, pm, ps, pt, bias_s, rate_s, skip_s, gated_o, ig_o, gm_o, gsh_o, gst_o, m):
    seq, mp = lax.axis_index("seq"), lax.axis_index("mp")
    core = lax.rem(mp, 2)
    chip = mp // 2
    partner = mp + 1 - 2 * core
    plane, line = seq // 4, lax.rem(seq, 4)
    low = lax.rem(seq, 2)

    load_tok = pltpu.make_async_copy(tok_hbm, m["tok3"], m["s_local"].at[0])
    load_cot = pltpu.make_async_copy(cot_hbm, m["cot"], m["s_local"].at[1])
    load_tok.start()
    load_cot.start()

    barrier = pltpu.get_barrier_semaphore()

    def greet_seq(d):
        pl.semaphore_signal(
            barrier, inc=1, device_id={"seq": lax.rem(seq + d, SEQ)}, device_id_type=MESH
        )

    def greet_mp(d):
        pl.semaphore_signal(barrier, inc=1, device_id={"mp": lax.rem(mp + d, MP)}, device_id_type=MESH)

    fori(1, SEQ, greet_seq)
    fori(1, MP, greet_mp)

    wa, wb, swp = m["wa"], m["wb"], m["swp"]
    wa[plane, line, :, pl.ds(0, 256)] = pm[:, 0, :]
    wb[plane, line, :, pl.ds(0, 256)] = pm[:, 1, :]
    wa[plane, line, :, pl.ds(256, 128)] = ps[:, 0, :]
    wb[plane, line, :, pl.ds(256, 128)] = ps[:, 1, :]
    at, lane = iota((SHARD, LANES), 0), iota((SHARD, LANES), 1)
    place = jnp.where(lane == at + SHARD * low, 1.0, 0.0).astype(BF)
    shifted = mm(pt[...], place).astype(BF)
    swp[...] = jnp.concatenate([shifted, shifted, jnp.zeros((8, LANES), BF)], axis=0)
    pl.semaphore_wait(barrier, SEQ + MP - 2)

    def along_x(k):
        return 4 * k + line

    def along_y(k):
        return 4 * plane + k

    half = SHARD // 2
    ring_a1 = Ring(plane, along_x, lambda k: wa.at[k, line], lambda k, n: wa.at[k, line, pl.ds(half * n, half)], m["s_w"].at[0])
    ring_b1 = Ring(line, along_y, lambda k: wb.at[plane, k], lambda k, n: wb.at[plane, k, pl.ds(half * n, half)], m["s_w"].at[1])
    ring_a2 = Ring(line, along_y, lambda k: wa.at[:, k], lambda k, n: wa.at[pl.ds(2 * n, 2), k], m["s_w"].at[2])
    ring_b2 = Ring(plane, along_x, lambda k: wb.at[k], lambda k, n: wb.at[k, pl.ds(2 * n, 2)], m["s_w"].at[3])
    rings = (ring_a1, ring_b1, ring_a2, ring_b2)
    ring_a1.start()
    ring_b1.start()
    send_sw = SeqExchange(lambda p: swp, lambda k: m["sw_rx"].at[k], sems(m["s_sw"]))
    send_sw.start()
    m["sw_rx"][seq] = swp[...]

    def flip(q):
        m["tokt"][:, pl.ds(q * CHUNK, CHUNK)] = m["tok3"][pl.ds(4 * q, 4)].reshape(CHUNK, DM).T

    load_tok.wait()
    flip(0)
    ring_a1.forward()
    ring_b1.forward()
    ring_a1.finish()
    ring_a2.start()
    ring_b1.finish()
    ring_b2.start()

    i, j = iota((CHUNK, CHUNK), 0), iota((CHUNK, CHUNK), 1)
    m["tri"][0] = jnp.where(i >= j, 1.0, 0.0).astype(BF)
    it, jt = (i & 15) * 16 + (i >> 4), (j & 15) * 16 + (j >> 4)
    m["tri"][1] = jnp.where(it >= jt, 1.0, 0.0).astype(BF)
    m["tri"][2] = jnp.where(i <= j, 1.0, 0.0).astype(BF)
    m["tri"][3] = jnp.where(it <= jt, 1.0, 0.0).astype(BF)
    m["sw"][...] = jnp.zeros((LANES, DM), BF)
    m["R"]["RC"][...] = jnp.zeros((8, INNER), F32)
    m["T"]["RC"][...] = jnp.zeros((8, INNER), F32)
    m["lacc"][...] = jnp.zeros((CHUNK, LANES), F32)

    head_l = iota((1, LANES), 1)
    head_c = iota((1, INNER), 1) >> 6

    def lanes_of(value):
        v = jnp.zeros((1, LANES), F32)
        for h in range(HEADS):
            v = jnp.where((head_l < 8) & ((head_l & 3) == h), value(h), v)
        return v

    def features_of(value):
        v = jnp.zeros((1, INNER), F32)
        for h in range(HEADS):
            v = jnp.where(head_c == h, value(h), v)
        return v

    bias = lanes_of(lambda h: bias_s[h])
    rate_r, rate_t = lanes_of(lambda h: rate_s[0, h]), lanes_of(lambda h: rate_s[1, h])
    ratex_r = features_of(lambda h: rate_s[0, h]) * LOG2E
    ratex_t = features_of(lambda h: rate_s[1, h]) * LOG2E
    skip = features_of(lambda h: skip_s[h])

    load_cot.wait()
    flip(1)
    ring_a2.forward()
    ring_b2.forward()
    flip(2)
    flip(3)
    ring_a2.finish()
    ring_b2.finish()
    send_sw.wait_recv()
    for k in range(SEQ // 2):
        m["sw"][pl.ds(0, 16), pl.ds(k * LANES, LANES)] = m["sw_rx"][2 * k] + m["sw_rx"][2 * k + 1]

    def rows_of(q):
        return pl.ds(pl.multiple_of(q * CHUNK, CHUNK), CHUNK)

    def columns(ref, at, width):
        return ref[:, :, :, pl.ds(at, width)].reshape(DM, width)

    def rest(v):
        return v.reshape(4, WID, LANES)

    send_pay = SeqExchange(lambda p: m["pay"].at[p], lambda k: m["trx"].at[k], sems(m["s_pay"]))
    quarter = pl.ds(pl.multiple_of(chip * COLS, COLS), COLS)
    bcr, bct = m["bcr"], m["bct"]
    send_bc = SeqExchange(
        lambda p: bcr.at[core, p, quarter], lambda k: bct.at[core, k, quarter], sems(m["s_bc"])
    )

    def piece_of(ref, k):
        return ref.at[lax.rem(k, 2), :, pl.ds(pl.multiple_of(k // 2 * COLS, COLS), COLS)]

    send_bm = MpExchange(lambda p: piece_of(bct, mp), lambda k: piece_of(bct, k), sems(m["s_bm"]))
    m["wx"][:, pl.ds(0, LANES)] = jnp.where(core == 0, columns(wa, 256, 128), columns(wb, 256, 128))
    m["wx"][:, pl.ds(LANES, LANES)] = m["sw"][...].T

    def start_four(exchange, q):
        def one(n):
            d = lax.rem(4 * q + n - seq + SEQ, SEQ)

            @pl.when(d != 0)
            def _():
                exchange.copy(d).start()

        fori(0, 4, one)

    def project_shared(n):
        q = lax.rem(plane + n, 4)
        u = m["tok3"][pl.ds(4 * q, 4)].reshape(CHUNK, DM)
        w = jnp.concatenate([columns(wa, 256, 128), columns(wb, 256, 128)], axis=1)
        v = mm(u, w).astype(BF)
        bcr[0, pl.ds(4 * q, 4)] = rest(v[:, :LANES])
        bcr[1, pl.ds(4 * q, 4)] = rest(v[:, LANES:])
        start_four(send_bc, q)

    def project(n):
        q = lax.rem(plane + n, 4)
        rows = rows_of(q)
        u = m["tok3"][pl.ds(4 * q, 4)].reshape(CHUNK, DM)
        four = pl.ds(4 * q, 4)

        def put(block, v):
            v = v.astype(BF)
            for k in range(v.shape[1] // LANES):
                m["pay"][four, pl.ds((block + k) * WID, WID), :] = rest(v[:, k * LANES : (k + 1) * LANES])

        z = mm(u, columns(wb, 0, 256)).astype(BF)
        m["z"][rows, :] = z
        zf = z.astype(F32)
        gate = zf * jax.nn.sigmoid(zf)
        put(BY, m["cot"][rows, :].astype(F32) * gate)
        put(BX, mm(u, columns(wa, 0, 256)))
        raw = mm(u, m["wx"][:, pl.ds(LANES, LANES)]) + bias
        m["sraw"][rows, :] = raw
        pair = as_pair(jnp.maximum(raw, 0.0) + jnp.log1p(jnp.exp(-jnp.abs(raw))))
        m["lp"][rows, :] = pair
        folded = jnp.zeros((64, LANES), F32)
        for g in range(4):
            part = rest(pair)[:, g * COLS : (g + 1) * COLS, :].reshape(64, LANES)
            folded += mm(part, pair_place(8 * g))
        m["pay"][four, pl.ds(ROWS_L, COLS), :] = folded.astype(BF).reshape(4, COLS, LANES)
        start_four(send_pay, q)

    fori(0, CHUNKS, project_shared)
    fori(0, CHUNKS, project)
    m["trx"][seq] = m["pay"][seq]
    bct[core, seq, quarter] = bcr[core, seq, quarter]

    def load_r(block, q):
        if block >= BB:
            return bcr[block - BB, pl.ds(4 * q, 4)].reshape(CHUNK, LANES)
        return m["pay"][pl.ds(4 * q, 4), pl.ds(block * WID, WID), :].reshape(CHUNK, LANES)

    def pair_r(q):
        return m["lp"][rows_of(q), :], 0

    def cols_of(block, q):
        return pl.ds(pl.multiple_of(block * WID + q * COLS, COLS), COLS)

    def load_t(block, q):
        if block >= BB:
            return bct[block - BB, :, pl.ds(q * COLS, COLS), :].reshape(CHUNK, LANES)
        return m["trx"][:, cols_of(block, q), :].reshape(CHUNK, LANES)

    def pair_t(q):
        return m["trx"][:, pl.ds(ROWS_L, COLS), :].reshape(CHUNK, LANES), 8 * q

    def pieces_exchange(source, landing, sem):
        return SeqExchange(lambda p: source.at[p], lambda k: landing.at[k], sems(sem))

    r, t = m["R"], m["T"]
    tri_r, tri_t, up_r, up_t = (m["tri"].at[k] for k in range(4))

    def chunks(low, high, step):
        for q in range(low, high):
            step(q)


    def start_pieces(b, sem):
        pack_states(b)
        e = pieces_exchange(b["st"], b["sx"], sem)
        e.start()
        b["sx"][seq] = b["st"][seq]
        return e

    def start_entering(b, sem):
        chain_states(b)
        e = pieces_exchange(b["sy"], b["sz"], sem)
        e.start()
        b["sz"][seq] = b["sy"][seq]
        return e

    chunks(0, CHUNKS, lambda q: summary(r, tri_r[...], load_r, pair_r, rate_r * LOG2E, ratex_r, q))
    send_sr = start_pieces(r, m["s_sr"])
    send_bc.wait_recv()
    send_bm.start()
    chunks(0, CHUNKS, lambda q: inside(r, tri_r[...], load_r, q))
    send_sr.wait_recv()
    send_ur = start_entering(r, m["s_ur"])

    send_pay.wait_recv()
    send_bm.wait_recv()
    chunks(0, CHUNKS, lambda q: summary(t, tri_t[...], load_t, pair_t, rate_t * LOG2E, ratex_t, q))
    send_st = start_pieces(t, m["s_st"])
    chunks(0, 2, lambda q: inside(t, tri_t[...], load_t, q))
    send_st.wait_recv()
    send_ut = start_entering(t, m["s_ut"])
    chunks(2, CHUNKS, lambda q: inside(t, tri_t[...], load_t, q))
    send_ut.wait_recv()
    entering_states(t)

    def put_t(q, y, dx, db, dc, dd):
        def put(block, v):
            v = v.astype(BF)
            for k in range(v.shape[1] // LANES):
                part = v[:, k * LANES : (k + 1) * LANES]
                at = 128 * (q // 2) + 32 * (block + k) + COLS * (q % 2)
                m["bpay"][:, pl.ds(at, COLS), :] = part.reshape(SEQ, COLS, LANES)

        put(BX, y)
        put(BY, dx)
        m["tdb"][0, q] = db.astype(BF)
        m["tdb"][1, q] = dc.astype(BF)
        for n in range(2):
            d = lax.rem(2 * q + n - mp + MP, MP)

            @pl.when(d != 0)
            def _():
                send_tr.copy(d).start()

        m["lacc"][...] += mm(as_pair(dd), pair_place(8 * q))

    def half_back(at, count, sem):
        rows = pl.ds(at, count)
        return SeqExchange(lambda p: m["bpay"].at[p, rows], lambda k: m["brx"].at[k, rows], sems(sem))

    send_back = half_back(0, 128, m["s_back"])
    send_back2 = half_back(128, 144, m["s_back2"])
    send_tr = MpExchange(
        lambda p: m["tdb"].at[lax.rem(p, 2), p // 2], lambda k: m["trs"].at[k], sems(m["s_tr"])
    )
    send_bp = SeqExchange(lambda p: m["tpiece"].at[p], lambda k: m["rpiece"].at[k], sems(m["s_bp"]))
    send_rr = MpExchange(lambda p: piece_of(m["rdb"], p), lambda k: m["rrs"].at[k], sems(m["s_rr"]))

    def group_total(ref):
        v = ref[0].astype(F32)
        for k in range(1, MP):
            v += ref[k].astype(F32)
        return v

    chunks(0, 2, lambda q: outside(t, tri_t[...], up_t[...], load_t, pair_t, rate_t, q, put_t))
    send_back.start()
    chunks(2, 4, lambda q: outside(t, tri_t[...], up_t[...], load_t, pair_t, rate_t, q, put_t))
    m["bpay"][:, pl.ds(ROWS_L, COLS), :] = m["lacc"][...].astype(BF).reshape(SEQ, COLS, LANES)
    send_back2.start()
    m["brx"][seq] = m["bpay"][seq]
    m["trs"][mp] = m["tdb"][core, chip]

    send_ur.wait_recv()
    entering_states(r)

    def put_r(q, y, dx, db, dc, dd):
        r["y"][q] = y
        r["dx"][q] = dx
        m["rdb"][0, pl.ds(4 * q, 4)] = rest(db.astype(BF))
        m["rdb"][1, pl.ds(4 * q, 4)] = rest(dc.astype(BF))
        r["dd"][q] = dd

    def outside_r(q):
        outside(r, tri_r[...], up_r[...], load_r, pair_r, rate_r, q, put_r)

    chunks(0, 1, outside_r)
    send_tr.wait_recv()
    m["tpiece"][...] = group_total(m["trs"]).astype(BF).reshape(SEQ, COLS, LANES)
    send_bp.start()
    m["rpiece"][seq] = m["tpiece"][seq]
    chunks(1, CHUNKS, outside_r)
    send_rr.start()
    m["rrs"][mp] = m["rdb"][core, :, quarter]
    send_back.wait_recv()
    send_back2.wait_recv()
    send_bp.wait_recv()
    send_rr.wait_recv()
    m["dpiece"][...] = (group_total(m["rrs"]) + m["rpiece"][...].astype(F32)).astype(BF)

    def back(block, q):
        parts = [m["brx"][pl.ds(4 * q, 4), pl.ds(128 * n + 32 * block, 32), :] for n in range(2)]
        return jnp.concatenate(parts, axis=1).reshape(CHUNK, LANES)

    def combine(q):
        rows = rows_of(q)
        x = wide(load_r, BX, q).astype(F32)
        dy = wide(load_r, BY, q).astype(F32)
        z = m["z"][rows, :].astype(F32)
        cot = m["cot"][rows, :].astype(F32)
        y = r["y"][q] + wide(back, BX, q).astype(F32) + skip * x
        sigma = jax.nn.sigmoid(z)
        gated_o[rows, :] = (y * (z * sigma)).astype(BF)
        m["g"][rows, pl.ds(256, 256)] = (cot * y * sigma * (1.0 + z * (1.0 - sigma))).astype(BF)
        m["g"][rows, pl.ds(0, 256)] = (r["dx"][q] + wide(back, BY, q).astype(F32) + skip * dy).astype(BF)
        folded = m["brx"][pl.ds(4 * q, 4), pl.ds(ROWS_L, COLS), :].reshape(64, LANES)
        parts = [mm(folded, pair_merge(8 * g)).reshape(4, COLS, LANES) for g in range(4)]
        dd = r["dd"][q] + jnp.concatenate(parts, axis=1).reshape(CHUNK, LANES)
        dstep = dd * jax.nn.sigmoid(m["sraw"][rows, :])
        m["g"][rows, pl.ds(640, LANES)] = jnp.where(iota((CHUNK, LANES), 1) < HEADS, dstep, 0.0).astype(BF)

    def pair_copy(k, q):
        rows = rows_of(q)
        return mp_copy(
            m["ip"].at[2 * k + 1 - core, rows],
            m["prx"].at[k, rows],
            m["s_pair"].at[0, k, q],
            m["s_pair"].at[1, k, q],
            partner,
        )

    def z_ring(n):
        def part(k, h):
            return m["zs"].at[k, pl.ds(CHUNK * (2 * n + h), CHUNK)]

        return RingSum(
            chip,
            lambda k: {"mp": 2 * k + core},
            part,
            lambda h: m["z_raw"].at[n, h],
            lambda side, h: m["z_near"].at[n, side, pl.ds(CHUNK * h, CHUNK)],
            m["s_z"].at[n],
        )

    z_rings = [z_ring(0), z_ring(1)]

    def pair_sum(k, q):
        rows = rows_of(q)
        pair_copy(k, q).wait_recv()
        return (m["ip"][2 * k + core, rows, :].astype(F32) + m["prx"][k, rows, :].astype(F32)).astype(BF)

    def pass_on(q):
        for k in range(4):
            m["zs"][k, rows_of(q), :] = pair_sum(k, q)

    def z_start(n):
        z_rings[n].start_far()
        z_rings[n].start_near()

    def z_finish(n):
        for h, v in enumerate(z_rings[n].finish()):
            ig_o[rows_of(2 * n + h), :] = v.astype(BF)

    def combine_all(q):
        combine(q)
        rows = rows_of(q)
        piece = m["dpiece"][pl.ds(4 * q, 4)]
        here = (iota((4, WID, LANES), 1) >> 4) == chip
        piece = jnp.where(here, jnp.concatenate([piece] * 4, axis=1), jnp.zeros((), BF)).reshape(CHUNK, LANES)
        m["g"][rows, pl.ds(512, LANES)] = piece

    def input_part(q):
        rows = rows_of(q)
        g = m["g"][rows, :]
        for c in range(4):
            cols = pl.ds(c * 256, 256)
            v = mm_nt(g[:, :256], wa[c, :, :, pl.ds(0, 256)].reshape(256, 256))
            v += mm_nt(g[:, 256:512], wb[c, :, :, pl.ds(0, 256)].reshape(256, 256))
            v += mm_nt(g[:, 512:], m["wx"][cols, :])
            v = v.astype(BF)
            m["ip"][2 * c, rows, :] = v[:, :LANES]
            m["ip"][2 * c + 1, rows, :] = v[:, LANES:]
        fori(0, 4, lambda k: pair_copy(k, q).start())

    chunks(0, CHUNKS, combine_all)

    def g_ring(n):
        rows = pl.ds(32 * n, 32)

        def part(k, h):
            two = pl.ds(2 * h, 2)
            return m["gp"].at[k, two, rows] if n == 0 else m["gp"].at[two, k, rows]

        return RingSum(
            plane if n == 0 else line,
            lambda k: {"seq": along_x(k) if n == 0 else along_y(k)},
            part,
            lambda h: m["g_raw"].at[n, h],
            lambda side, h: m["g_near"].at[n, side, pl.ds(2 * h, 2)],
            m["s_gp"].at[n],
        )

    def h_ring(n):
        return RingSum(
            line if n == 0 else plane,
            lambda k: {"seq": along_y(k) if n == 0 else along_x(k)},
            lambda k, h: m["h_own"].at[n, k, pl.ds(16 * h, 16)],
            lambda h: m["h_raw"].at[n, h],
            lambda side, h: m["h_near"].at[n, side, pl.ds(16 * h, 16)],
            m["s_gp"].at[2 + n],
        )

    g_rings, h_rings = [g_ring(0), g_ring(1)], [h_ring(0), h_ring(1)]
    send_gs = SeqExchange(lambda p: m["gs"].at[p // 2], lambda k: m["gs_rx"].at[k], sems(m["s_gs"]))

    def grads(n):
        k = lax.rem(plane + n, 4)
        cols = rows_of(k)
        v = mm(m["tokt"][cols, :], m["g"][...])
        m["gp"][k] = v[:, :640].astype(BF).reshape(4, SHARD, 640)
        gs = v[:, 640:].T[:16].astype(BF)
        m["gs"][2 * k] = gs[:, :LANES]
        m["gs"][2 * k + 1] = gs[:, LANES:]
        start_four(send_gs, k)

    grads(2)
    g_rings[0].start_far()
    grads(1)
    grads(3)
    g_rings[0].start_near()
    grads(0)
    g_rings[1].start_far()
    g_rings[1].start_near()
    m["gs_rx"][seq] = m["gs"][seq // 2]
    input_part(0)
    input_part(1)
    g_rings[0].middle()
    g_rings[1].middle()
    pass_on(0)
    pass_on(1)
    z_start(0)
    input_part(2)
    input_part(3)

    def g_next(n):
        for h, v in enumerate(g_rings[n].finish()):
            m["h_own"][n, pl.ds(2 * h, 2)] = v.astype(BF).reshape(2, 32, 640)
        h_rings[n].start_far()
        h_rings[n].start_near()

    g_next(0)
    g_next(1)
    pass_on(2)
    pass_on(3)
    z_start(1)
    z_rings[0].middle()
    h_rings[0].middle()
    h_rings[1].middle()
    z_rings[1].middle()

    def total_of(ref):
        v = ref[0].astype(F32)
        for k in range(1, SEQ):
            v += ref[k].astype(F32)
        return v

    main = jnp.concatenate(h_rings[0].finish() + h_rings[1].finish(), axis=0)
    m["fsh"][...] = main[:, 512:]
    send_fin = MpExchange(lambda p: m["fsh"], lambda k: m["frx"].at[k], sems(m["s_fin"]))
    send_fin.start()
    m["frx"][mp] = main[:, 512:]
    gm_o[:, 0, :] = main[:, :INNER]
    gm_o[:, 1, :] = main[:, INNER : 2 * INNER]
    send_gs.wait_recv()
    step = total_of(m["gs_rx"])
    gst_o[...] = jnp.where(low == 0, step[:HEADS, :SHARD], step[:HEADS, SHARD:])
    z_finish(0)
    z_finish(1)
    send_fin.wait_recv()
    for n in range(2):
        gsh_o[:, n, :] = m["frx"][n] + m["frx"][2 + n] + m["frx"][4 + n] + m["frx"][6 + n]

    sent = rings + (send_sw, send_pay, send_bc, send_bm, send_sr, send_ur, send_st, send_ut)
    sent += (send_back, send_back2, send_tr, send_bp, send_rr, send_gs, send_fin)
    sent += tuple(z_rings + g_rings + h_rings)
    for e in sent:
        e.wait_send()
    for q in range(CHUNKS):
        fori(0, 4, lambda k: pair_copy(k, q).wait_send())


def hand_over(*refs):
    n = len(refs) // 2
    for k in range(n):
        refs[n + k][...] = refs[k][...]


def body(tokens, proj_main, proj_shared, proj_step, step_bias, decay_rate, skip_gain, cotangent):
    vm = pl.BlockSpec(memory_space=pltpu.VMEM)
    sm = pl.BlockSpec(memory_space=pltpu.SMEM)
    hbm = pl.BlockSpec(memory_space=pl.ANY)
    shapes = (
        jax.ShapeDtypeStruct((TOK, INNER), BF),
        jax.ShapeDtypeStruct((TOK, LANES), BF),
        jax.ShapeDtypeStruct((SHARD, 2, INNER), F32),
        jax.ShapeDtypeStruct((SHARD, 2, STATE), F32),
        jax.ShapeDtypeStruct((HEADS, SHARD), F32),
    )
    results = pl.pallas_call(
        kernel,
        out_shape=shapes,
        in_specs=[hbm, hbm, vm, vm, vm, sm, sm, sm],
        out_specs=(vm,) * 5,
        scratch_shapes=[main_scratch()],
        compiler_params=pltpu.CompilerParams(
            collective_id=0, has_side_effects=True, vmem_limit_bytes=62 * 1024 * 1024
        ),
    )(
        tokens.reshape(SEQ, WID, DM),
        cotangent.reshape(TOK, INNER),
        proj_main,
        proj_shared,
        proj_step.T,
        step_bias,
        decay_rate,
        skip_gain,
    )
    gated, ig, gm, gsh, gst = pl.pallas_call(
        hand_over,
        out_shape=shapes,
        in_specs=[vm] * 5,
        out_specs=(vm,) * 5,
    )(*results)
    return (
        gated.reshape(1, 16, WID, INNER),
        ig.reshape(1, 16, WID, LANES),
        gm,
        gsh,
        gst.T,
    )


def solution(mesh):
    placed = (
        P("seq", None, None, None),
        P("seq", None, "mp"),
        P("seq", None, None),
        P("seq", "mp"),
        P("mp"),
        P(None, "mp"),
        P("mp"),
        P("seq", None, None, "mp"),
    )
    return jax.shard_map(
        body,
        mesh=mesh,
        in_specs=placed,
        out_specs=(
            P("seq", None, None, "mp"),
            P("seq", None, None, "mp"),
            P("seq", None, "mp"),
            P("seq", None, None),
            P("seq", "mp"),
        ),
        check_vma=False,
    )
```

profile of v0, /device:TPU:1, one launch (start us, length us, event | category | flops | bytes accessed | tf_op | source)
XLA Modules:
  0.0 110.7 jit_solution(7625870814489660084)
XLA Ops:
  0.6 107.9 %shard_map.119 = (bf16[1024,256]{1,0:T(8,128)(2,1)}, bf16[1024,128]{1,0:T(8,128)(2,1)}, f32[64,2,256]{2,1,0:T(2,128)}, f32[64,2,128]{2,1,0:T(2,128)}, f32[4,64]{1,0:T(4,128)}) custom-call(bf16[16,64,1024]{2,1,0:T(8,128)(2,1)} %bitcast.6, bf16[1024,256]{1,0:T(8,128)(2,1)} %bitcast.7, bf16[64,2,256]{2,1,0:T(2,128)(2,1)} %pm.1, bf16[64,2,128]{2,1,0:T(2,128)(2,1)} %ps.1, ...), custom_call_target="tpu_custom_call" | custom-call | tf_op jit(solution)/shard_map/pallas_call | solution.py:1028
  108.6 2.1 %shard_map.120 = (bf16[1024,256]{1,0:T(8,128)(2,1)}, bf16[1024,128]{1,0:T(8,128)(2,1)}, f32[64,2,256]{2,1,0:T(2,128)}, f32[64,2,128]{2,1,0:T(2,128)}, f32[4,64]{1,0:T(4,128)}) custom-call(bf16[1024,256]{1,0:T(8,128)(2,1)} %get-tuple-element.15.refs_0_, bf16[1024,128]{1,0:T(8,128)(2,1)} %get-tuple-element.16.refs_1_, ...), custom_call_target="tpu_custom_call" | custom-call | tf_op jit(solution)/shard_map/pallas_call | solution.py:1047
where the time goes:
time: 111 us
  Pallas kernels  110 us (99%)
    pallas_call x1, Pallas kernels, body(): pl.pallas_call(kernel, out_shape=shapes, in_specs=[hbm, hbm, vm, vm, vm,...  108 us

commit v1 on v0

--- a/solution.py
+++ b/solution.py
@@ -64,8 +64,8 @@
 
 
 class SeqExchange:
-    def __init__(self, source, landing, sems):
-        self.source, self.landing = source, landing
+    def __init__(self, source, landing, many, sems):
+        self.source, self.landing, self.many = source, landing, many
         self.send, self.recv = sems
         self.me = lax.axis_index("seq")
 
@@ -74,31 +74,34 @@
         return pltpu.make_async_remote_copy(
             src_ref=self.source(peer),
             dst_ref=self.landing(self.me),
-            send_sem=self.send.at[d],
-            recv_sem=self.recv.at[d],
+            send_sem=self.send,
+            recv_sem=self.recv,
             device_id={"seq": peer},
             device_id_type=MESH,
         )
 
-    def arrival(self, d):
-        origin = lax.rem(self.me - d + SEQ, SEQ)
+    def all(self):
         return pltpu.make_async_remote_copy(
-            src_ref=self.landing(origin),
-            dst_ref=self.landing(origin),
-            send_sem=self.send.at[d],
-            recv_sem=self.recv.at[d],
-            device_id={"seq": origin},
+            src_ref=self.many,
+            dst_ref=self.many,
+            send_sem=self.send,
+            recv_sem=self.recv,
+            device_id={"seq": lax.rem(self.me + 1, SEQ)},
             device_id_type=MESH,
         )
 
     def start(self):
-        fori(1, SEQ, lambda d: self.copy(d).start())
+        def one(i):
+            step = i // 2
+            self.copy(SEQ // 2 + jnp.where(lax.rem(i, 2) == 0, step, -step)).start()
+
+        fori(1, SEQ, one)
 
     def wait_recv(self):
-        fori(1, SEQ, lambda d: self.arrival(d).wait_recv())
+        self.all().wait_recv()
 
     def wait_send(self):
-        fori(1, SEQ, lambda d: self.copy(d).wait_send())
+        self.all().wait_send()
 
 
 class Ring:
@@ -262,7 +265,7 @@
 def main_scratch():
     v = pltpu.VMEM
     dma = pltpu.SemaphoreType.DMA
-    seq_sems = lambda: dma((2, SEQ))
+    seq_sems = lambda: dma((2,))
     return dict(
         tok3=v((SEQ, WID, DM), BF),
         cot=v((TOK, INNER), BF),
@@ -531,6 +534,8 @@
     swp[...] = jnp.concatenate([shifted, shifted, jnp.zeros((8, LANES), BF)], axis=0)
     pl.semaphore_wait(barrier, SEQ + MP - 2)
 
+    most = pl.ds(0, SEQ - 1)
+
     def along_x(k):
         return 4 * k + line
 
@@ -545,7 +550,7 @@
     rings = (ring_a1, ring_b1, ring_a2, ring_b2)
     ring_a1.start()
     ring_b1.start()
-    send_sw = SeqExchange(lambda p: swp, lambda k: m["sw_rx"].at[k], sems(m["s_sw"]))
+    send_sw = SeqExchange(lambda p: swp, lambda k: m["sw_rx"].at[k], m["sw_rx"].at[most], sems(m["s_sw"]))
     send_sw.start()
     m["sw_rx"][seq] = swp[...]
 
@@ -614,11 +619,14 @@
     def rest(v):
         return v.reshape(4, WID, LANES)
 
-    send_pay = SeqExchange(lambda p: m["pay"].at[p], lambda k: m["trx"].at[k], sems(m["s_pay"]))
+    send_pay = SeqExchange(lambda p: m["pay"].at[p], lambda k: m["trx"].at[k], m["trx"].at[most], sems(m["s_pay"]))
     quarter = pl.ds(pl.multiple_of(chip * COLS, COLS), COLS)
     bcr, bct = m["bcr"], m["bct"]
     send_bc = SeqExchange(
-        lambda p: bcr.at[core, p, quarter], lambda k: bct.at[core, k, quarter], sems(m["s_bc"])
+        lambda p: bcr.at[core, p, quarter],
+        lambda k: bct.at[core, k, quarter],
+        bct.at[core, most, quarter],
+        sems(m["s_bc"]),
     )
 
     def piece_of(ref, k):
@@ -638,8 +646,12 @@
 
         fori(0, 4, one)
 
+    def far_first(n):
+        step = jnp.where(n == 0, 2, jnp.where(n == 3, 0, 2 * n - 1))
+        return lax.rem(plane + step, 4)
+
     def project_shared(n):
-        q = lax.rem(plane + n, 4)
+        q = far_first(n)
         u = m["tok3"][pl.ds(4 * q, 4)].reshape(CHUNK, DM)
         w = jnp.concatenate([columns(wa, 256, 128), columns(wb, 256, 128)], axis=1)
         v = mm(u, w).astype(BF)
@@ -648,7 +660,7 @@
         start_four(send_bc, q)
 
     def project(n):
-        q = lax.rem(plane + n, 4)
+        q = far_first(n)
         rows = rows_of(q)
         u = m["tok3"][pl.ds(4 * q, 4)].reshape(CHUNK, DM)
         four = pl.ds(4 * q, 4)
@@ -700,7 +712,7 @@
         return m["trx"][:, pl.ds(ROWS_L, COLS), :].reshape(CHUNK, LANES), 8 * q
 
     def pieces_exchange(source, landing, sem):
-        return SeqExchange(lambda p: source.at[p], lambda k: landing.at[k], sems(sem))
+        return SeqExchange(lambda p: source.at[p], lambda k: landing.at[k], landing.at[most], sems(sem))
 
     r, t = m["R"], m["T"]
     tri_r, tri_t, up_r, up_t = (m["tri"].at[k] for k in range(4))
@@ -711,7 +723,6 @@
 
 
     def start_pieces(b, sem):
-        pack_states(b)
         e = pieces_exchange(b["st"], b["sx"], sem)
         e.start()
         b["sx"][seq] = b["st"][seq]
@@ -725,21 +736,28 @@
         return e
 
     chunks(0, CHUNKS, lambda q: summary(r, tri_r[...], load_r, pair_r, rate_r * LOG2E, ratex_r, q))
-    send_sr = start_pieces(r, m["s_sr"])
+    pack_states(r)
     send_bc.wait_recv()
     send_bm.start()
-    chunks(0, CHUNKS, lambda q: inside(r, tri_r[...], load_r, q))
+    chunks(0, 2, lambda q: inside(r, tri_r[...], load_r, q))
+    send_sw.wait_send()
+    for e in rings:
+        e.wait_send()
+
+    send_pay.wait_recv()
+    send_sr = start_pieces(r, m["s_sr"])
+    send_bm.wait_recv()
+    chunks(0, CHUNKS, lambda q: summary(t, tri_t[...], load_t, pair_t, rate_t * LOG2E, ratex_t, q))
+    pack_states(t)
+    send_st = start_pieces(t, m["s_st"])
     send_sr.wait_recv()
     send_ur = start_entering(r, m["s_ur"])
-
-    send_pay.wait_recv()
-    send_bm.wait_recv()
-    chunks(0, CHUNKS, lambda q: summary(t, tri_t[...], load_t, pair_t, rate_t * LOG2E, ratex_t, q))
-    send_st = start_pieces(t, m["s_st"])
     chunks(0, 2, lambda q: inside(t, tri_t[...], load_t, q))
+    chunks(2, 3, lambda q: inside(r, tri_r[...], load_r, q))
     send_st.wait_recv()
     send_ut = start_entering(t, m["s_ut"])
     chunks(2, CHUNKS, lambda q: inside(t, tri_t[...], load_t, q))
+    chunks(3, CHUNKS, lambda q: inside(r, tri_r[...], load_r, q))
     send_ut.wait_recv()
     entering_states(t)
 
@@ -766,14 +784,16 @@
 
     def half_back(at, count, sem):
         rows = pl.ds(at, count)
-        return SeqExchange(lambda p: m["bpay"].at[p, rows], lambda k: m["brx"].at[k, rows], sems(sem))
+        return SeqExchange(
+            lambda p: m["bpay"].at[p, rows], lambda k: m["brx"].at[k, rows], m["brx"].at[most, rows], sems(sem)
+        )
 
     send_back = half_back(0, 128, m["s_back"])
     send_back2 = half_back(128, 144, m["s_back2"])
     send_tr = MpExchange(
         lambda p: m["tdb"].at[lax.rem(p, 2), p // 2], lambda k: m["trs"].at[k], sems(m["s_tr"])
     )
-    send_bp = SeqExchange(lambda p: m["tpiece"].at[p], lambda k: m["rpiece"].at[k], sems(m["s_bp"]))
+    send_bp = SeqExchange(lambda p: m["tpiece"].at[p], lambda k: m["rpiece"].at[k], m["rpiece"].at[most], sems(m["s_bp"]))
     send_rr = MpExchange(lambda p: piece_of(m["rdb"], p), lambda k: m["rrs"].at[k], sems(m["s_rr"]))
 
     def group_total(ref):
@@ -811,6 +831,8 @@
     chunks(1, CHUNKS, outside_r)
     send_rr.start()
     m["rrs"][mp] = m["rdb"][core, :, quarter]
+    for e in (send_pay, send_bc, send_bm, send_sr, send_ur, send_st, send_ut):
+        e.wait_send()
     send_back.wait_recv()
     send_back2.wait_recv()
     send_bp.wait_recv()
@@ -930,7 +952,7 @@
         )
 
     g_rings, h_rings = [g_ring(0), g_ring(1)], [h_ring(0), h_ring(1)]
-    send_gs = SeqExchange(lambda p: m["gs"].at[p // 2], lambda k: m["gs_rx"].at[k], sems(m["s_gs"]))
+    send_gs = SeqExchange(lambda p: m["gs"].at[p // 2], lambda k: m["gs_rx"].at[k], m["gs_rx"].at[most], sems(m["s_gs"]))
 
     def grads(n):
         k = lax.rem(plane + n, 4)
@@ -960,6 +982,8 @@
     z_start(0)
     input_part(2)
     input_part(3)
+    for e in (send_back, send_back2, send_tr, send_bp, send_rr, send_gs):
+        e.wait_send()
 
     def g_next(n):
         for h, v in enumerate(g_rings[n].finish()):
@@ -999,9 +1023,7 @@
     for n in range(2):
         gsh_o[:, n, :] = m["frx"][n] + m["frx"][2 + n] + m["frx"][4 + n] + m["frx"][6 + n]
 
-    sent = rings + (send_sw, send_pay, send_bc, send_bm, send_sr, send_ur, send_st, send_ut)
-    sent += (send_back, send_back2, send_tr, send_bp, send_rr, send_gs, send_fin)
-    sent += tuple(z_rings + g_rings + h_rings)
+    sent = [send_fin] + z_rings + g_rings + h_rings
     for e in sent:
         e.wait_send()
     for q in range(CHUNKS):

time: 111 us -> 107 us (0.964)
  Pallas kernels: 110 us -> 106 us
    pallas_call x1, Pallas kernels: 108 us -> 104 us  [body(): pl.pallas_call(kernel, out_shape=shapes, in_specs=[hbm, hbm, vm, vm, vm,...]
where the time goes in v1:
time: 107 us
  Pallas kernels  106 us (99%)
    pallas_call x1, Pallas kernels, body(): pl.pallas_call(kernel, out_shape=shapes, in_specs=[hbm, hbm, vm, vm, vm,...  104 us

profile of v1, /device:TPU:1, one launch (start us, length us, event | category | flops | bytes accessed | tf_op | source)
XLA Modules:
  0.0 107.0 jit_solution(13532972184667292070)
XLA Ops:
  0.6 104.2 %shard_map.119 = (bf16[1024,256]{1,0:T(8,128)(2,1)}, bf16[1024,128]{1,0:T(8,128)(2,1)}, f32[64,2,256]{2,1,0:T(2,128)}, f32[64,2,128]{2,1,0:T(2,128)}, f32[4,64]{1,0:T(4,128)}) custom-call(bf16[16,64,1024]{2,1,0:T(8,128)(2,1)} %bitcast.6, bf16[1024,256]{1,0:T(8,128)(2,1)} %bitcast.7, bf16[64,2,256]{2,1,0:T(2,128)(2,1)} %pm.1, bf16[64,2,128]{2,1,0:T(2,128)(2,1)} %ps.1, ...), custom_call_target="tpu_custom_call" | custom-call | tf_op jit(solution)/shard_map/pallas_call | solution.py:1050
  104.9 2.1 %shard_map.120 = (bf16[1024,256]{1,0:T(8,128)(2,1)}, bf16[1024,128]{1,0:T(8,128)(2,1)}, f32[64,2,256]{2,1,0:T(2,128)}, f32[64,2,128]{2,1,0:T(2,128)}, f32[4,64]{1,0:T(4,128)}) custom-call(bf16[1024,256]{1,0:T(8,128)(2,1)} %get-tuple-element.15.refs_0_, bf16[1024,128]{1,0:T(8,128)(2,1)} %get-tuple-element.16.refs_1_, ...), custom_call_target="tpu_custom_call" | custom-call | tf_op jit(solution)/shard_map/pallas_call | solution.py:1069

commit v2 on v1

--- a/solution.py
+++ b/solution.py
@@ -275,6 +275,8 @@
         sw=v((LANES, DM), BF),
         z=v((TOK, INNER), BF),
         sraw=v((TOK, LANES), F32),
+        gate=v((TOK, INNER), F32),
+        slope=v((TOK, INNER), F32),
         pay=v((SEQ, ROWS, LANES), BF),
         trx=v((SEQ, ROWS, LANES), BF),
         bpay=v((SEQ, ROWS, LANES), BF),
@@ -814,8 +816,14 @@
     entering_states(r)
 
     def put_r(q, y, dx, db, dc, dd):
-        r["y"][q] = y
-        r["dx"][q] = dx
+        rows = rows_of(q)
+        r["y"][q] = y + skip * wide(load_r, BX, q).astype(F32)
+        r["dx"][q] = dx + skip * wide(load_r, BY, q).astype(F32)
+        z = m["z"][rows, :].astype(F32)
+        sigma = jax.nn.sigmoid(z)
+        m["gate"][rows, :] = z * sigma
+        m["slope"][rows, :] = m["cot"][rows, :].astype(F32) * sigma * (1.0 + z * (1.0 - sigma))
+        m["sraw"][rows, :] = jax.nn.sigmoid(m["sraw"][rows, :])
         m["rdb"][0, pl.ds(4 * q, 4)] = rest(db.astype(BF))
         m["rdb"][1, pl.ds(4 * q, 4)] = rest(dc.astype(BF))
         r["dd"][q] = dd
@@ -845,19 +853,14 @@
 
     def combine(q):
         rows = rows_of(q)
-        x = wide(load_r, BX, q).astype(F32)
-        dy = wide(load_r, BY, q).astype(F32)
-        z = m["z"][rows, :].astype(F32)
-        cot = m["cot"][rows, :].astype(F32)
-        y = r["y"][q] + wide(back, BX, q).astype(F32) + skip * x
-        sigma = jax.nn.sigmoid(z)
-        gated_o[rows, :] = (y * (z * sigma)).astype(BF)
-        m["g"][rows, pl.ds(256, 256)] = (cot * y * sigma * (1.0 + z * (1.0 - sigma))).astype(BF)
-        m["g"][rows, pl.ds(0, 256)] = (r["dx"][q] + wide(back, BY, q).astype(F32) + skip * dy).astype(BF)
+        y = r["y"][q] + wide(back, BX, q).astype(F32)
+        gated_o[rows, :] = (y * m["gate"][rows, :]).astype(BF)
+        m["g"][rows, pl.ds(256, 256)] = (y * m["slope"][rows, :]).astype(BF)
+        m["g"][rows, pl.ds(0, 256)] = (r["dx"][q] + wide(back, BY, q).astype(F32)).astype(BF)
         folded = m["brx"][pl.ds(4 * q, 4), pl.ds(ROWS_L, COLS), :].reshape(64, LANES)
         parts = [mm(folded, pair_merge(8 * g)).reshape(4, COLS, LANES) for g in range(4)]
         dd = r["dd"][q] + jnp.concatenate(parts, axis=1).reshape(CHUNK, LANES)
-        dstep = dd * jax.nn.sigmoid(m["sraw"][rows, :])
+        dstep = dd * m["sraw"][rows, :]
         m["g"][rows, pl.ds(640, LANES)] = jnp.where(iota((CHUNK, LANES), 1) < HEADS, dstep, 0.0).astype(BF)
 
     def pair_copy(k, q):
@@ -977,13 +980,16 @@
     input_part(1)
     g_rings[0].middle()
     g_rings[1].middle()
+    input_part(2)
     pass_on(0)
     pass_on(1)
     z_start(0)
-    input_part(2)
     input_part(3)
     for e in (send_back, send_back2, send_tr, send_bp, send_rr, send_gs):
         e.wait_send()
+    pass_on(2)
+    pass_on(3)
+    z_start(1)
 
     def g_next(n):
         for h, v in enumerate(g_rings[n].finish()):
@@ -993,9 +999,6 @@
 
     g_next(0)
     g_next(1)
-    pass_on(2)
-    pass_on(3)
-    z_start(1)
     z_rings[0].middle()
     h_rings[0].middle()
     h_rings[1].middle()

time: 107 us -> 107 us (level)
  no operation moved by 1% of the time
where the time goes in v2:
time: 107 us
  Pallas kernels  106 us (99%)
    pallas_call x1, Pallas kernels, body(): pl.pallas_call(kernel, out_shape=shapes, in_specs=[hbm, hbm, vm, vm, vm,...  104 us

profile of v2, /device:TPU:1, one launch (start us, length us, event | category | flops | bytes accessed | tf_op | source)
XLA Modules:
  0.0 106.6 jit_solution(16536994796729850889)
XLA Ops:
  0.6 103.9 %shard_map.119 = (bf16[1024,256]{1,0:T(8,128)(2,1)}, bf16[1024,128]{1,0:T(8,128)(2,1)}, f32[64,2,256]{2,1,0:T(2,128)}, f32[64,2,128]{2,1,0:T(2,128)}, f32[4,64]{1,0:T(4,128)}) custom-call(bf16[16,64,1024]{2,1,0:T(8,128)(2,1)} %bitcast.6, bf16[1024,256]{1,0:T(8,128)(2,1)} %bitcast.7, bf16[64,2,256]{2,1,0:T(2,128)(2,1)} %pm.1, bf16[64,2,128]{2,1,0:T(2,128)(2,1)} %ps.1, ...), custom_call_target="tpu_custom_call" | custom-call | tf_op jit(solution)/shard_map/pallas_call | solution.py:1053
  104.5 2.1 %shard_map.120 = (bf16[1024,256]{1,0:T(8,128)(2,1)}, bf16[1024,128]{1,0:T(8,128)(2,1)}, f32[64,2,256]{2,1,0:T(2,128)}, f32[64,2,128]{2,1,0:T(2,128)}, f32[4,64]{1,0:T(4,128)}) custom-call(bf16[1024,256]{1,0:T(8,128)(2,1)} %get-tuple-element.15.refs_0_, bf16[1024,128]{1,0:T(8,128)(2,1)} %get-tuple-element.16.refs_1_, ...), custom_call_target="tpu_custom_call" | custom-call | tf_op jit(solution)/shard_map/pallas_call | solution.py:1072

commit v3 on v2

--- a/solution.py
+++ b/solution.py
@@ -755,11 +755,9 @@
     send_sr.wait_recv()
     send_ur = start_entering(r, m["s_ur"])
     chunks(0, 2, lambda q: inside(t, tri_t[...], load_t, q))
-    chunks(2, 3, lambda q: inside(r, tri_r[...], load_r, q))
     send_st.wait_recv()
     send_ut = start_entering(t, m["s_ut"])
     chunks(2, CHUNKS, lambda q: inside(t, tri_t[...], load_t, q))
-    chunks(3, CHUNKS, lambda q: inside(r, tri_r[...], load_r, q))
     send_ut.wait_recv()
     entering_states(t)
 
@@ -812,6 +810,12 @@
     m["brx"][seq] = m["bpay"][seq]
     m["trs"][mp] = m["tdb"][core, chip]
 
+    inside(r, tri_r[...], load_r, 2)
+    send_tr.wait_recv()
+    m["tpiece"][...] = group_total(m["trs"]).astype(BF).reshape(SEQ, COLS, LANES)
+    send_bp.start()
+    m["rpiece"][seq] = m["tpiece"][seq]
+    inside(r, tri_r[...], load_r, 3)
     send_ur.wait_recv()
     entering_states(r)
 
@@ -831,12 +835,7 @@
     def outside_r(q):
         outside(r, tri_r[...], up_r[...], load_r, pair_r, rate_r, q, put_r)
 
-    chunks(0, 1, outside_r)
-    send_tr.wait_recv()
-    m["tpiece"][...] = group_total(m["trs"]).astype(BF).reshape(SEQ, COLS, LANES)
-    send_bp.start()
-    m["rpiece"][seq] = m["tpiece"][seq]
-    chunks(1, CHUNKS, outside_r)
+    chunks(0, CHUNKS, outside_r)
     send_rr.start()
     m["rrs"][mp] = m["rdb"][core, :, quarter]
     for e in (send_pay, send_bc, send_bm, send_sr, send_ur, send_st, send_ut):

time: 107 us -> 108 us (level)
  Pallas kernels: 106 us -> 108 us
    pallas_call x1, Pallas kernels: 104 us -> 105 us  [body(): pl.pallas_call(kernel, out_shape=shapes, in_specs=[hbm, hbm, vm, vm, vm,...]
where the time goes in v3:
time: 108 us
  Pallas kernels  108 us (100%)
    pallas_call x1, Pallas kernels, body(): pl.pallas_call(kernel, out_shape=shapes, in_specs=[hbm, hbm, vm, vm, vm,...  105 us

profile of v3, /device:TPU:1, one launch (start us, length us, event | category | flops | bytes accessed | tf_op | source)
XLA Modules:
  0.0 108.2 jit_solution(11768705130840165074)
XLA Ops:
  0.6 105.4 %shard_map.119 = (bf16[1024,256]{1,0:T(8,128)(2,1)}, bf16[1024,128]{1,0:T(8,128)(2,1)}, f32[64,2,256]{2,1,0:T(2,128)}, f32[64,2,128]{2,1,0:T(2,128)}, f32[4,64]{1,0:T(4,128)}) custom-call(bf16[16,64,1024]{2,1,0:T(8,128)(2,1)} %bitcast.6, bf16[1024,256]{1,0:T(8,128)(2,1)} %bitcast.7, bf16[64,2,256]{2,1,0:T(2,128)(2,1)} %pm.1, bf16[64,2,128]{2,1,0:T(2,128)(2,1)} %ps.1, ...), custom_call_target="tpu_custom_call" | custom-call | tf_op jit(solution)/shard_map/pallas_call | solution.py:1052
  106.0 2.1 %shard_map.120 = (bf16[1024,256]{1,0:T(8,128)(2,1)}, bf16[1024,128]{1,0:T(8,128)(2,1)}, f32[64,2,256]{2,1,0:T(2,128)}, f32[64,2,128]{2,1,0:T(2,128)}, f32[4,64]{1,0:T(4,128)}) custom-call(bf16[1024,256]{1,0:T(8,128)(2,1)} %get-tuple-element.15.refs_0_, bf16[1024,128]{1,0:T(8,128)(2,1)} %get-tuple-element.16.refs_1_, ...), custom_call_target="tpu_custom_call" | custom-call | tf_op jit(solution)/shard_map/pallas_call | solution.py:1071

commit v4 on v2

--- a/solution.py
+++ b/solution.py
@@ -742,6 +742,15 @@
     send_bc.wait_recv()
     send_bm.start()
     chunks(0, 2, lambda q: inside(r, tri_r[...], load_r, q))
+    def gates(q):
+        rows = rows_of(q)
+        z = m["z"][rows, :].astype(F32)
+        sigma = jax.nn.sigmoid(z)
+        m["gate"][rows, :] = z * sigma
+        m["slope"][rows, :] = m["cot"][rows, :].astype(F32) * sigma * (1.0 + z * (1.0 - sigma))
+        m["sraw"][rows, :] = jax.nn.sigmoid(m["sraw"][rows, :])
+
+    chunks(0, CHUNKS, gates)
     send_sw.wait_send()
     for e in rings:
         e.wait_send()
@@ -819,11 +828,6 @@
         rows = rows_of(q)
         r["y"][q] = y + skip * wide(load_r, BX, q).astype(F32)
         r["dx"][q] = dx + skip * wide(load_r, BY, q).astype(F32)
-        z = m["z"][rows, :].astype(F32)
-        sigma = jax.nn.sigmoid(z)
-        m["gate"][rows, :] = z * sigma
-        m["slope"][rows, :] = m["cot"][rows, :].astype(F32) * sigma * (1.0 + z * (1.0 - sigma))
-        m["sraw"][rows, :] = jax.nn.sigmoid(m["sraw"][rows, :])
         m["rdb"][0, pl.ds(4 * q, 4)] = rest(db.astype(BF))
         m["rdb"][1, pl.ds(4 * q, 4)] = rest(dc.astype(BF))
         r["dd"][q] = dd

time: 107 us -> 106 us (level)
  no operation moved by 1% of the time
where the time goes in v4:
time: 106 us
  Pallas kernels  106 us (100%)
    pallas_call x1, Pallas kernels, body(): pl.pallas_call(kernel, out_shape=shapes, in_specs=[hbm, hbm, vm, vm, vm,...  103 us
    pallas_call x1, Pallas kernels, body(): pl.pallas_call(hand_over, out_shape=shapes, in_specs=[vm] * 5, out_specs=...  2.13 us

profile of v4, /device:TPU:1, one launch (start us, length us, event | category | flops | bytes accessed | tf_op | source)
XLA Modules:
  0.0 106.2 jit_solution(10360621471374600260)
XLA Ops:
  0.6 103.4 %shard_map.119 = (bf16[1024,256]{1,0:T(8,128)(2,1)}, bf16[1024,128]{1,0:T(8,128)(2,1)}, f32[64,2,256]{2,1,0:T(2,128)}, f32[64,2,128]{2,1,0:T(2,128)}, f32[4,64]{1,0:T(4,128)}) custom-call(bf16[16,64,1024]{2,1,0:T(8,128)(2,1)} %bitcast.6, bf16[1024,256]{1,0:T(8,128)(2,1)} %bitcast.7, bf16[64,2,256]{2,1,0:T(2,128)(2,1)} %pm.1, bf16[64,2,128]{2,1,0:T(2,128)(2,1)} %ps.1, ...), custom_call_target="tpu_custom_call" | custom-call | tf_op jit(solution)/shard_map/pallas_call | solution.py:1057
  104.1 2.1 %shard_map.120 = (bf16[1024,256]{1,0:T(8,128)(2,1)}, bf16[1024,128]{1,0:T(8,128)(2,1)}, f32[64,2,256]{2,1,0:T(2,128)}, f32[64,2,128]{2,1,0:T(2,128)}, f32[4,64]{1,0:T(4,128)}) custom-call(bf16[1024,256]{1,0:T(8,128)(2,1)} %get-tuple-element.15.refs_0_, bf16[1024,128]{1,0:T(8,128)(2,1)} %get-tuple-element.16.refs_1_, ...), custom_call_target="tpu_custom_call" | custom-call | tf_op jit(solution)/shard_map/pallas_call | solution.py:1076
